TPU v7x, 32 devices: a whole 2x2x4 slice. The times are simulated.
32 devices in a mesh: grid: 8 (over z, y), slab: 4 (over x, core).
Axes of the slice: x: 2, y: 2, z: 4, core: 2. Of those that a mesh axis runs over, the one named last changes fastest.
Arguments:
- support: bfloat16 [64, 4, 32, 1024], P('grid', None, 'slab'), may hold values from -0.359375 to 0.359375
- potential: bfloat16 [256, 512], P(('grid', 'slab')), may hold values from -6 to 6
- kernel: float32 [64, 4, 4], P('grid'), may hold values from -18 to 18
- block_list: int32 [64, 4, 16], P('grid', 'slab'), may hold values from 0 to 255, as said below
Outputs:
- applied: bfloat16 [64, 4, 32, 1024], P('grid', None, 'slab')
- density: float32 [256, 512], P(('grid', 'slab'))
- hamiltonian: float32 [64, 4, 4], P('grid')
Inputs may be any that keep to these rules, and one draw needn't show every extreme that they name: (block_list[a, l, j] // 8) % 4 == l. Within one layer, the 8 atoms of one grid index name blocks with any one value of block // 32 at most 32 times, and exactly 32 times for some value.
All inputs are finite; a program needn't handle non-finite values.
Results may differ from a plain program's by a relative error of at most 0.0004.
Values may be sent and summed in bfloat16 or wider, within the bound.
A program may use at most 64 MiB of HBM per device.

v0:
```python
import jax
import jax.numpy as jnp
from jax import lax
from jax.sharding import PartitionSpec as P

FUNCS = 4
BOX = 32
BLOCK = 8
RADIUS = 13
SIDE_BLOCKS = 4
SLOTS = 16


STENCIL_WEIGHTS = (
    -5369.0 / 1800.0,
    12.0 / 7.0,
    -15.0 / 56.0,
    10.0 / 189.0,
    -1.0 / 112.0,
    2.0 / 1925.0,
    -1.0 / 16632.0,
)
CELL_VOLUME = 0.125
KINETIC_FACTOR = 2.0


def extended(array, sides, width):
    for axis, dim in sides:
        peers, length = (lax.axis_size(axis), array.shape[dim])
        up = [(i, (i + 1) % peers) for i in range(peers - 1)]
        down = [(j, i) for i, j in up]
        last = lax.slice_in_dim(array, length - width, length, axis=dim)
        leading = lax.slice_in_dim(array, 0, width, axis=dim)
        before = lax.ppermute(last, axis, up)
        after = lax.ppermute(leading, axis, down)
        array = jnp.concatenate([before, array, after], axis=dim)
    return array


def stencil_sum(centre, padded, start, stride, length, direction):
    stencil_reach = len(STENCIL_WEIGHTS) - 1
    summed = STENCIL_WEIGHTS[0] * centre
    for offset in range(1, stencil_reach + 1):
        forward = lax.slice_in_dim(
            padded, start + offset * stride, start + offset * stride + length, axis=direction
        )
        backward = lax.slice_in_dim(
            padded, start - offset * stride, start - offset * stride + length, axis=direction
        )
        summed = summed + STENCIL_WEIGHTS[offset] * (forward + backward)
    return summed


def serve_blocks(potential, asked_ids):
    return jnp.take(potential, jnp.maximum(asked_ids - 1, 0), axis=0)


def collect_density(potential, incoming_blocks, incoming_parts):
    block_count = potential.shape[0]
    matches = (
        incoming_blocks.reshape(1, -1) - 1 == jnp.arange(block_count, dtype=jnp.int32)[:, None]
    ).astype(jnp.float32)
    return jnp.dot(
        matches,
        incoming_parts.reshape(-1, incoming_parts.shape[-1]),
        precision=lax.Precision.HIGHEST,
    )


def per_device(support, potential, kernel, block_list):
    atom_count = support.shape[0]
    planes = support.shape[2]
    plane_cells = support.shape[3]
    stencil_reach = len(STENCIL_WEIGHTS) - 1
    grid_count = lax.axis_size("grid")
    slab_count = lax.axis_size("slab")
    block_count = potential.shape[0]
    block_cells = potential.shape[1]
    depth_index = planes * lax.axis_index("slab") + jnp.arange(planes, dtype=jnp.int32)
    depth_square = (2 * depth_index - (BOX - 1)) ** 2
    cell_index = jnp.arange(plane_cells, dtype=jnp.int32)
    row_square = (2 * (cell_index // BOX) - (BOX - 1)) ** 2
    column_square = (2 * (cell_index % BOX) - (BOX - 1)) ** 2
    inside = depth_square[:, None] + (row_square + column_square)[None, :] <= (2 * RADIUS) ** 2
    masked = jnp.where(inside[None, None], support, jnp.zeros((), jnp.bfloat16))
    rimmed = extended(masked, (("slab", 2),), stencil_reach)
    field_values = masked.astype(jnp.float32)
    field_flat = field_values.reshape(atom_count, FUNCS, planes * plane_cells)
    mixed_field = jnp.einsum("afg,agp->afp", kernel, field_flat, precision=lax.Precision.HIGHEST)
    deposit = jnp.sum(field_flat * mixed_field, axis=1)
    deposit = deposit.reshape(atom_count, planes, SIDE_BLOCKS, BLOCK, SIDE_BLOCKS, BLOCK)
    deposit_rows = jnp.transpose(deposit, (0, 2, 4, 1, 3, 5)).reshape(
        atom_count * SLOTS, block_cells
    )
    wanted = block_list.reshape(-1)
    request_count = wanted.shape[0]
    capacity = max(2, 2 * request_count // grid_count)
    peer_index = wanted // (slab_count * block_count)
    local_block = wanted % block_count
    member = (peer_index[:, None] == jnp.arange(grid_count, dtype=jnp.int32)[None, :]).astype(
        jnp.int32
    )
    rank_index = jnp.sum(member * jnp.cumsum(member, axis=0), axis=1) - 1
    slot_index = peer_index * capacity + rank_index
    outgoing_blocks = (
        jnp.zeros((grid_count * capacity,), jnp.int32).at[slot_index].set(local_block + 1)
    )
    outgoing_blocks = outgoing_blocks.reshape(grid_count, capacity)
    outgoing_parts = (
        jnp.zeros((grid_count * capacity, block_cells), jnp.float32)
        .at[slot_index]
        .set(deposit_rows)
    )
    outgoing_parts = outgoing_parts.reshape(grid_count, capacity, block_cells)
    returned = lax.all_to_all(
        serve_blocks(
            potential,
            lax.all_to_all(outgoing_blocks, "grid", split_axis=0, concat_axis=0, tiled=True),
        ),
        "grid",
        split_axis=0,
        concat_axis=0,
        tiled=True,
    )
    potential_rows = jnp.take(returned.reshape(-1, block_cells), slot_index, axis=0)
    incoming_blocks, incoming_parts = (
        lax.all_to_all(outgoing_blocks, "grid", split_axis=0, concat_axis=0, tiled=True),
        lax.all_to_all(outgoing_parts, "grid", split_axis=0, concat_axis=0, tiled=True),
    )
    density = collect_density(potential, incoming_blocks, incoming_parts)
    potential_box = potential_rows.reshape(
        atom_count, SIDE_BLOCKS, SIDE_BLOCKS, BLOCK, BLOCK, BLOCK
    )
    potential_box = jnp.transpose(potential_box, (0, 3, 1, 4, 2, 5)).reshape(
        atom_count, planes, plane_cells
    )
    rimmed_field = rimmed.astype(jnp.float32)
    along_depth = stencil_sum(field_values, rimmed_field, stencil_reach, 1, planes, 2)
    wide_rows = jnp.pad(
        field_values, ((0, 0), (0, 0), (0, 0), (stencil_reach * BOX, stencil_reach * BOX))
    )
    along_rows = stencil_sum(field_values, wide_rows, stencil_reach * BOX, BOX, plane_cells, 3)
    wide_columns = jnp.pad(field_values, ((0, 0), (0, 0), (0, 0), (stencil_reach, stencil_reach)))
    along_columns = stencil_sum(field_values, wide_columns, stencil_reach, 1, plane_cells, 3)
    laplace = along_depth + along_rows + along_columns
    applied_full = jnp.where(
        inside[None, None],
        -KINETIC_FACTOR * laplace + potential_box.astype(jnp.float32)[:, None] * field_values,
        0.0,
    )
    applied = applied_full.astype(jnp.bfloat16)
    local_matrix = jnp.einsum(
        "afp,agp->afg",
        field_flat,
        applied_full.reshape(atom_count, FUNCS, -1),
        precision=lax.Precision.HIGHEST,
    )
    hamiltonian = lax.psum(local_matrix, "slab") * CELL_VOLUME
    return (applied, density, hamiltonian)


def solution(mesh):
    in_specs = (
        P("grid", None, "slab", None),
        P(("grid", "slab"), None),
        P("grid", None, None),
        P("grid", "slab", None),
    )
    out_specs = (P("grid", None, "slab", None), P(("grid", "slab"), None), P("grid", None, None))
    return jax.shard_map(
        per_device, mesh=mesh, in_specs=in_specs, out_specs=out_specs, check_vma=False
    )
```

profile of v0, /device:TPU:0, one launch (start us, length us, event | category | flops | bytes accessed | tf_op | source)
XLA Modules:
  0.0 114.8 jit_solution(6659397228346660109)
XLA Ops:
  1.2 1.3 %reduce.5 = s32[8,16]{1,0:T(8,128)S(1)} reduce(s32[8,1,16]{2,1,0:T(1,128)} %param.7, s32[]{:T(128)} %broadcast.417), dimensions={1}, to_apply=%param.7.reduce_sub_computation.5 | reduce | bytes 1028 | tf_op args[3]
  3.8 1.0 scatter_custom_fusion
  5.5 7.3 %all-to-all-start = ((s32[8,1,32]{2,1,0:T(1,128)}), s32[8,1,32]{2,1,0:T(1,128)S(1)}, u32[]{:S(2)}, u32[]{:S(2)}) async-start(s32[8,1,32]{2,1,0:T(1,128)} %all_to_all.13), calls=%async_computation | async-start | bytes 8192 | tf_op jit(solution)/shard_map/all_to_all | solution.py:118
  12.9 2.2 %fusion.84 = (f32[8,4,8,1024]{3,2,1,0:T(8,128)}, bf16[8,4,8,1024]{3,2,1,0:T(8,128)(2,1)S(1)}) fusion(bf16[8,4,8,1024]{3,2,1,0:T(8,128)(2,1)} %param.4, pred[8,1024]{1,0:T(8,128)(4,1)S(1)} %add_compare_fusion), kind=kLoop, calls=%fused_computation.158 | loop fusion | flops 524288 | bytes 2105344 | tf_op jit(solution)/shard_map/convert_element_type | solution.py:87
  15.1 1.1 fusion.85
  16.2 1.5 %collective-permute-start = (bf16[8,4,6,1024]{3,2,1,0:T(8,128)(2,1)}, bf16[8,4,6,1024]{3,2,1,0:T(8,128)(2,1)S(1)}, u32[]{:S(2)}, u32[]{:S(2)}) collective-permute-start(bf16[8,4,6,1024]{3,2,1,0:T(8,128)(2,1)} %get-tuple-element.22), channel_id=1, source_target_pairs={{0,1},{1,2},{2,3},{4,5},{5,6},{6,7},{8,9},{9,10},{10,11},{12,13},{... | collective-permute-start | bytes 1179656 | tf_op jit(solution)/shard_map/ppermute | solution.py:34
  17.7 1.3 %collective-permute-start.1 = (bf16[8,4,6,1024]{3,2,1,0:T(8,128)(2,1)}, bf16[8,4,6,1024]{3,2,1,0:T(8,128)(2,1)}, u32[]{:S(2)}, u32[]{:S(2)}) collective-permute-start(bf16[8,4,6,1024]{3,2,1,0:T(8,128)(2,1)} %get-tuple-element.23), channel_id=1, source_target_pairs={{1,0},{2,1},{3,2},{5,4},{6,5},{7,6},{9,8},{10,9},{11,10},{13,12},{... | collective-permute-start | bytes 1179656 | tf_op jit(solution)/shard_map/ppermute | solution.py:35
  21.5 1.2 %gather_fusion = bf16[256,512]{1,0:T(8,128)(2,1)S(1)} fusion(bf16[8,512]{1,0:T(8,128)(2,1)S(1)} %copy-done, s32[1024]{0:T(1024)S(1)} %pad_clamp_fusion.1), kind=kCustom, calls=%fused_computation | custom fusion | bytes 525312 | tf_op jit(solution)/shard_map/jit(_take)/gather | solution.py:55
  23.5 5.8 %all-to-all-start.1 = ((bf16[8,32,512]{2,1,0:T(8,128)(2,1)}), bf16[8,32,512]{2,1,0:T(8,128)(2,1)S(1)}, u32[]{:S(2)}, u32[]{:S(2)}) async-start(bf16[8,32,512]{2,1,0:T(8,128)(2,1)} %broadcast_select_fusion.1), calls=%async_computation.1 | async-start | bytes 524288 | tf_op jit(solution)/shard_map/all_to_all | solution.py:115
  29.3 1.6 %fusion.1 = f32[8,8192]{1,0:T(8,128)S(1)} fusion(f32[8,4,8192]{2,1,0:T(4,128)S(1)} %reshape.274, bf16[8,4,8192]{2,1,0:T(4,128)(2,1)S(1)} %reshape.275, f32[8,4,4]{2,1,0:T(4,128)S(1)} %copy.37), kind=kOutput, calls=%fused_computation.21 | convolution fusion | flops 13041664 | bytes 1835520 | tf_op jit(solution)/shard_map/afg,agp->afp/dot_general | solution.py:89
  30.9 6.9 %reshape.276 = f32[8,8,4,8,4,8]{5,4,3,2,1,0:T(4,128)} reshape(f32[8,8192]{1,0:T(8,128)S(1)} %fusion.1) | data formatting | bytes 524288 | tf_op jit(solution)/shard_map/reshape | solution.py:91
  37.8 4.8 %copy.38 = f32[8,4,4,8,8,8]{5,4,3,2,1,0:T(8,128)} copy(f32[8,4,4,8,8,8]{5,2,4,1,3,0:T(4,128)} %bitcast.41) | data formatting | bytes 524288 | tf_op jit(solution)/shard_map/transpose | solution.py:92
  42.6 4.0 %reshape.310 = f32[128,512]{1,0:T(8,128)S(1)} reshape(f32[8,4,4,8,8,8]{5,4,3,2,1,0:T(8,128)} %copy.38) | data formatting | bytes 524288 | tf_op jit(solution)/shard_map/reshape | solution.py:92
  46.5 1.8 %scatter_custom_fusion.1 = f32[256,512]{1,0:T(8,128)} fusion(s32[128]{0:T(128)S(1)} %fusion.79, f32[128,512]{1,0:T(8,128)S(1)} %reshape.310, f32[]{:T(128)} %constant.131.clone.1), kind=kCustom, calls=%fused_computation.94 | custom fusion | bytes 524292 | tf_op jit(solution)/shard_map/scatter | solution.py:112
  50.4 2.1 %maximum_convert_fusion = f32[8,4,20,1024]{3,2,1,0:T(8,128)S(1)} fusion(bf16[8,4,6,1024]{3,2,1,0:T(8,128)(2,1)} %collective-permute-done.1, bf16[8,4,8,1024]{3,2,1,0:T(8,128)(2,1)} %copy-done.1, bf16[8,4,6,1024]{3,2,1,0:T(8,128)(2,1)} %copy-done.2), kind=kLoop, calls=%fused_computation.20 | loop fusion | flops 3932160 | bytes 3932160 | tf_op jit(solution)/shard_map/convert_element_type | solution.py:137
  52.5 6.0 %all-to-all-start.2 = ((f32[8,32,512]{2,1,0:T(8,128)}), f32[8,32,512]{2,1,0:T(8,128)}, u32[]{:S(2)}, u32[]{:S(2)}) async-start(f32[8,32,512]{2,1,0:T(8,128)} %bitcast.43), calls=%async_computation.2 | async-start | bytes 1048576 | tf_op jit(solution)/shard_map/all_to_all | solution.py:128
  59.5 3.5 %gather.12 = bf16[8,4,4,8,8,8]{5,4,3,2,1,0:T(8,128)(2,1)} reshape(bf16[128,512]{1,0:T(8,128)(2,1)S(1)} %gather_fusion.1) | data formatting | bytes 262144 | tf_op jit(solution)/shard_map/jit(_take)/gather | solution.py:125
  62.9 5.0 %convert_bitcast_fusion = f32[8,8,4,8,4,8]{5,4,3,2,1,0:T(4,128)} fusion(bf16[8,4,4,8,8,8]{5,4,3,2,1,0:T(8,128)(2,1)} %gather.12, pred[8,4,4]{2,1,0:T(4,128)(4,1)} %copy.34), kind=kLoop, calls=%fused_computation.6 | loop fusion | flops 131072 | bytes 393344 | tf_op jit(solution)/shard_map/convert_element_type | solution.py:148
  67.9 6.6 %reshape.281 = f32[8,8,1024]{2,1,0:T(8,128)S(1)} reshape(f32[8,8,4,8,4,8]{5,4,3,2,1,0:T(4,128)} %convert_bitcast_fusion) | data formatting | bytes 524288 | tf_op jit(solution)/shard_map/convert_element_type | solution.py:148
  74.5 19.6 %fusion.82 = (bf16[8,4,8,1024]{3,2,1,0:T(8,128)(2,1)}, f32[8,4,8,1024]{3,2,1,0:T(8,128)}) fusion(f32[8,4,8,1024]{3,2,1,0:T(8,128)} %get-tuple-element.20, f32[8,8,1024]{2,1,0:T(8,128)S(1)} %reshape.281, f32[8,4,20,1024]{3,2,1,0:T(8,128)S(1)} %maximum_convert_fusion, pred[8,1024]{1,0:T(8,128)(4,1)S(1)} %add_compare_fusion), kind=kLoop, calls=%fused_computation.157 | loop fusion | flops 16252928 | bytes 15474688 | tf_op jit(solution)/shard_map/convert_element_type | solution.py:151
  94.2 1.9 %reshape.280 = f32[8,4,8192]{2,1,0:T(4,128)S(1)} reshape(f32[8,4,8,1024]{3,2,1,0:T(8,128)} %get-tuple-element.19) | data formatting | bytes 2097152 | tf_op jit(solution)/shard_map/reshape | solution.py:155
  96.1 3.3 %fusion.86 = f32[8,4,4]{2,1,0:T(4,128)S(1)} fusion(bf16[8,4,8192]{2,1,0:T(4,128)(2,1)} %copy-done.3, f32[8,4,8192]{2,1,0:T(4,128)S(1)} %reshape.280), kind=kOutput, calls=%fused_computation.160 | convolution fusion | flops 12582912 | bytes 1573376 | tf_op jit(solution)/shard_map/afp,agp->afg/dot_general | solution.py:152
  99.3 12.8 %psum.7 = f32[8,4,4]{2,1,0:T(4,128)S(1)} all-reduce(f32[8,4,4]{2,1,0:T(4,128)S(1)} %fusion.86), channel_id=1, replica_groups=mesh['grid'=8,'slab'=4] {'slab'}, use_global_device_ids=true, to_apply=%region_5.6 | all-reduce | flops 128 | bytes 1024 | tf_op jit(solution)/shard_map/psum | solution.py:158
  112.8 1.9 %fusion.66 = f32[8,512]{1,0:T(8,128)} fusion(f32[256,512]{1,0:T(8,128)} %bitcast.11, s32[256]{0:T(256)S(1)} %copy-done.6), kind=kOutput, calls=%fused_computation.120 | convolution fusion | flops 12584960 | bytes 541696 | tf_op jit(solution)/shard_map/dot_general | solution.py:63
  (50 shorter events, 9.6 us)
Async XLA Ops:
  0.6 20.9 %copy-start = (bf16[8,512]{1,0:T(8,128)(2,1)S(1)}, bf16[8,512]{1,0:T(8,128)(2,1)}, u32[]{:S(2)}) copy-start(bf16[8,512]{1,0:T(8,128)(2,1)} %param.5) | copy-start | bytes 24580
  0.6 18.4 %copy-start.4 = (s32[8,1,16]{2,1,0:T(1,128)S(1)}, s32[8,1,16]{2,1,0:T(1,128)}, u32[]{:S(2)}) copy-start(s32[8,1,16]{2,1,0:T(1,128)} %param.7) | copy-start | bytes 1540
  5.5 15.9 %all-to-all-start = ((s32[8,1,32]{2,1,0:T(1,128)}), s32[8,1,32]{2,1,0:T(1,128)S(1)}, u32[]{:S(2)}, u32[]{:S(2)}) async-start(s32[8,1,32]{2,1,0:T(1,128)} %all_to_all.13), calls=%async_computation | async-start | bytes 8192 | tf_op jit(solution)/shard_map/all_to_all | solution.py:118
  12.9 8.4 %copy-start.5 = (f32[8,4,4]{0,2,1:T(4,128)S(1)}, f32[8,4,4]{0,2,1:T(4,128)}, u32[]{:S(2)}) copy-start(f32[8,4,4]{0,2,1:T(4,128)} %param.6) | copy-start | bytes 1540
  15.1 7.6 %copy-start.1 = (bf16[8,4,8,1024]{3,2,1,0:T(8,128)(2,1)}, bf16[8,4,8,1024]{3,2,1,0:T(8,128)(2,1)S(1)}, u32[]{:S(2)}) copy-start(bf16[8,4,8,1024]{3,2,1,0:T(8,128)(2,1)S(1)} %get-tuple-element.21) | copy-start | bytes 1572868
  16.2 33.3 %collective-permute-start = (bf16[8,4,6,1024]{3,2,1,0:T(8,128)(2,1)}, bf16[8,4,6,1024]{3,2,1,0:T(8,128)(2,1)S(1)}, u32[]{:S(2)}, u32[]{:S(2)}) collective-permute-start(bf16[8,4,6,1024]{3,2,1,0:T(8,128)(2,1)} %get-tuple-element.22), channel_id=1, source_target_pairs={{0,1},{1,2},{2,3},{4,5},{5,6},{6,7},{8,9},{9,10},{10,11},{12,13},{... | collective-permute-start | bytes 1179656 | tf_op jit(solution)/shard_map/ppermute | solution.py:34
  17.7 32.7 %collective-permute-start.1 = (bf16[8,4,6,1024]{3,2,1,0:T(8,128)(2,1)}, bf16[8,4,6,1024]{3,2,1,0:T(8,128)(2,1)}, u32[]{:S(2)}, u32[]{:S(2)}) collective-permute-start(bf16[8,4,6,1024]{3,2,1,0:T(8,128)(2,1)} %get-tuple-element.23), channel_id=1, source_target_pairs={{1,0},{2,1},{3,2},{5,4},{6,5},{7,6},{9,8},{10,9},{11,10},{13,12},{... | collective-permute-start | bytes 1179656 | tf_op jit(solution)/shard_map/ppermute | solution.py:35
  19.8 11.1 %copy-start.3 = (bf16[8,4,8192]{2,1,0:T(4,128)(2,1)}, bf16[8,4,8192]{2,1,0:T(4,128)(2,1)S(1)}, u32[]{:S(2)}) copy-start(bf16[8,4,8192]{2,1,0:T(4,128)(2,1)S(1)} %reshape.275) | copy-start | bytes 1572868
  23.5 29.0 %all-to-all-start.1 = ((bf16[8,32,512]{2,1,0:T(8,128)(2,1)}), bf16[8,32,512]{2,1,0:T(8,128)(2,1)S(1)}, u32[]{:S(2)}, u32[]{:S(2)}) async-start(bf16[8,32,512]{2,1,0:T(8,128)(2,1)} %broadcast_select_fusion.1), calls=%async_computation.1 | async-start | bytes 524288 | tf_op jit(solution)/shard_map/all_to_all | solution.py:115
  49.6 0.8 copy-start.2
  52.5 60.3 %all-to-all-start.2 = ((f32[8,32,512]{2,1,0:T(8,128)}), f32[8,32,512]{2,1,0:T(8,128)}, u32[]{:S(2)}, u32[]{:S(2)}) async-start(f32[8,32,512]{2,1,0:T(8,128)} %bitcast.43), calls=%async_computation.2 | async-start | bytes 1048576 | tf_op jit(solution)/shard_map/all_to_all | solution.py:128
  94.1 18.7 %copy-start.6 = (s32[256]{0:T(256)S(1)}, s32[256]{0:T(256)}, u32[]{:S(2)}) copy-start(s32[256]{0:T(256)} %sub.51) | copy-start | bytes 3076
where the time goes:
time: 115 us
  local copies, waits for them, and re-layouts  40.2 us (35%)
  other arithmetic  32.2 us (28%)
  starting transfers between devices  21.9 us (19%)
  blocking collectives  12.8 us (11%)
  matrix products  6.75 us (6%)
    convert_element_type x1, other arithmetic, per_device(): applied = applied_full.astype(jnp.bfloat16)  19.6 us
    psum x1, blocking collectives, per_device(): hamiltonian = lax.psum(local_matrix, 'slab') * CELL_VOLUME  12.8 us
    all_to_all x1, starting transfers between devices, per_device(): lax.all_to_all(outgoing_blocks, 'grid', split_axis=0, concat_axis=0, tile...  7.28 us
    reshape x1, local copies, waits for them, and re-layouts, per_device(): deposit.reshape(atom_count, planes, SIDE_BLOCKS, BLOCK, SIDE_BLOCKS, BLOCK)  6.89 us
    convert_element_type x1, local copies, waits for them, and re-layouts, per_device(): potential_box.astype(jnp.float32)[:, None] * field_values  6.58 us
    all_to_all x1, starting transfers between devices, per_device(): lax.all_to_all(outgoing_parts, 'grid', split_axis=0, concat_axis=0, tiled...  6.02 us
    all_to_all x1, starting transfers between devices, per_device(): lax.all_to_all(serve_blocks(potential, lax.all_to_all(outgoing_blocks, 'g...  5.82 us
    convert_element_type x1, other arithmetic, per_device(): potential_box.astype(jnp.float32)[:, None] * field_values  4.99 us
  transfers between devices with their start and end apart: 5, of which 0 were waited for; matrix products, arithmetic and copies ran while one was open for 62% of the time, Pallas kernels for 0%

commit v1 on v0

v1 whole, which is shorter than its diff:
```python
import functools

import jax
import jax.numpy as jnp
import ml_dtypes
import numpy as np
from jax import lax
from jax.experimental import pallas as pl
from jax.experimental.pallas import tpu as pltpu
from jax.sharding import PartitionSpec as P

FUNCS = 4
BOX = 32
BLOCK = 8
RADIUS = 13
SIDE = 4
REACH = 6
TILE = 256
WEIGHTS = (
    -5369.0 / 1800.0,
    12.0 / 7.0,
    -15.0 / 56.0,
    10.0 / 189.0,
    -1.0 / 112.0,
    2.0 / 1925.0,
    -1.0 / 16632.0,
)
CELL_VOLUME = 0.125
KINETIC = -2.0
MESH = pl.DeviceIdType.MESH
F32 = jnp.float32
BF16 = jnp.bfloat16


def split(array):
    high = array.astype(ml_dtypes.bfloat16)
    low = (array - high.astype(np.float64)).astype(ml_dtypes.bfloat16)
    return high, low


def band(offset):
    weight = np.zeros(offset.shape)
    for k in range(1, REACH + 1):
        weight = np.where(np.abs(offset) == k, WEIGHTS[k], weight)
    return KINETIC * weight


def constants(rows):
    lane = np.arange(TILE)
    y, z = lane // BOX, lane % BOX
    parts = []
    for shift in (-BLOCK, 0, BLOCK):
        from_y = (y + shift)[:, None]
        matrix = band(y[None] - from_y) * (z[:, None] == z[None])
        if shift == 0:
            matrix = matrix + band(z[None] - z[:, None]) * (y[:, None] == y[None])
            matrix = matrix + 3 * KINETIC * WEIGHTS[0] * np.eye(TILE)
        parts.extend(split(matrix))
    plane = np.concatenate(parts, axis=0)

    row = np.arange(rows)
    pair, x = row // BLOCK, row % BLOCK
    halo = np.arange(rows // BLOCK * REACH)
    halo_pair, halo_x = halo // REACH, halo % REACH
    same = pair[:, None] == halo_pair[None]
    before = band(x[:, None] - (halo_x - REACH)[None]) * same
    after = band(x[:, None] - (halo_x + BLOCK)[None]) * same
    centre = band(x[:, None] - x[None]) * (pair[:, None] == pair[None])
    depth = np.concatenate(split(np.concatenate([centre, before, after], axis=1)), axis=0)

    up = (halo_x + BLOCK - REACH)[:, None] == x[None]
    down = halo_x[:, None] == x[None]
    select = np.concatenate([up & same.T, down & same.T], axis=0)

    spot = np.arange(128)
    half, cell = spot // 64, spot % 64
    match = (cell // 8)[:, None] == y[None]
    match = match & ((cell % 8)[:, None] == (z % 8)[None])
    spread = np.concatenate([match & (half == h)[:, None] for h in (0, 1)], axis=1)

    column = np.arange(SIDE * 128)
    slot, side, goal = column // 128, column % 128 // 64, column % 64
    here = (y[:, None] == (goal // 8)[None]) & (z[:, None] == (slot * 8 + goal % 8)[None])
    gather = np.concatenate([here & (side == h)[None] for h in (0, 1)], axis=0)

    to = ml_dtypes.bfloat16
    return plane, depth, select.astype(to), spread.astype(to), gather.astype(to)


def dot(a, b, dims=((1,), (0,)), precision=None):
    return lax.dot_general(
        a, b, (dims, ((), ())), precision=precision, preferred_element_type=F32
    )


def kernel_body(
    n, s, atoms, blocks,
    sup_hbm, pot, ker, bl, plane_hbm, depth_hbm, select_hbm, spread_hbm, gather_hbm,
    applied, density, ham,
    sup, plane, depth, select, spread, gather,
    field, fieldb, pre, halo_out, halo, pot_own, pot_all, dep_rows, dep_out, dep_in,
    ham_own, ham_all,
    load_sem, halo_send, halo_recv, pot_send, pot_recv, dep_send, dep_recv,
    ham_send, ham_recv,
):
    rows = atoms * FUNCS * BLOCK
    edge = rows // BLOCK * REACH
    part = blocks * 4
    me_g, me_s = lax.axis_index("grid"), lax.axis_index("slab")

    loads = [
        pltpu.make_async_copy(src, dst, load_sem.at[i])
        for i, (src, dst) in enumerate(
            (
                (sup_hbm, sup), (select_hbm, select), (gather_hbm, gather),
                (spread_hbm, spread), (plane_hbm, plane), (depth_hbm, depth),
            )
        )
    ]
    for load in loads:
        load.start()

    barrier = pltpu.get_barrier_semaphore()

    def greet(k, carry):
        pl.semaphore_signal(
            barrier, inc=1, device_id=(lax.rem(me_g + k, n), me_s), device_id_type=MESH
        )
        return carry

    lax.fori_loop(1, n, greet, 0)
    for k in range(1, s):
        pl.semaphore_signal(
            barrier, inc=1, device_id=(me_g, lax.rem(me_s + k, s)), device_id_type=MESH
        )

    own = pot[...].astype(F32)
    for c in range(4):
        dep_rows[c * blocks : (c + 1) * blocks, 0:128] = own[:, c * 128 : (c + 1) * 128]
    pot_own[...] = dep_rows[0:part, 0:128].astype(BF16)
    pot_all[pl.ds(me_g, 1)] = pot_own[...][None]

    x2 = 2 * (me_s * BLOCK + lax.broadcasted_iota(jnp.int32, (BLOCK, 1), 0)) - (BOX - 1)
    cells = lax.broadcasted_iota(jnp.int32, (1, BOX * BOX), 1)
    y2 = 2 * (cells // BOX) - (BOX - 1)
    z2 = 2 * (cells % BOX) - (BOX - 1)
    inside = (x2 * x2 + (y2 * y2 + z2 * z2)) <= (2 * RADIUS) ** 2
    loads[0].wait()
    for j in range(SIDE):
        lanes = slice(j * TILE, (j + 1) * TILE)
        values = sup[:, lanes].astype(F32).reshape(atoms * FUNCS, BLOCK, TILE)
        values = jnp.where(inside[None, :, lanes], values, 0.0).reshape(rows, TILE)
        field[:, lanes] = values
        fieldb[:, lanes] = values.astype(BF16)
    loads[1].wait()
    for j in range(SIDE):
        lanes = slice(j * TILE, (j + 1) * TILE)
        halo_out[j] = dot(select[...], fieldb[:, lanes]).astype(BF16)

    pl.semaphore_wait(barrier, n - 1 + s - 1)

    def pot_copy(k):
        return pltpu.make_async_remote_copy(
            src_ref=pot_own,
            dst_ref=pot_all.at[me_g],
            send_sem=pot_send,
            recv_sem=pot_recv,
            device_id=(lax.rem(me_g + k, n), me_s),
            device_id_type=MESH,
        )

    def send_pot(k, carry):
        pot_copy(k).start()
        return carry

    lax.fori_loop(1, n, send_pot, 0)

    def halo_copy(j, direction):
        first = direction * edge
        return pltpu.make_async_remote_copy(
            src_ref=halo_out.at[j, pl.ds(first, edge)],
            dst_ref=halo.at[j, pl.ds(first, edge)],
            send_sem=halo_send.at[direction, j],
            recv_sem=halo_recv.at[direction, j],
            device_id=(me_g, me_s + 1 - 2 * direction),
            device_id_type=MESH,
        )

    has_after, has_before = me_s < s - 1, me_s > 0

    @pl.when(has_after)
    def _():
        for j in range(SIDE):
            halo_copy(j, 0).start()

    @pl.when(has_before)
    def _():
        for j in range(SIDE):
            halo_copy(j, 1).start()

    @pl.when(jnp.logical_not(has_after))
    def _():
        halo[:, edge:, :] = jnp.zeros((SIDE, edge, TILE), BF16)

    @pl.when(jnp.logical_not(has_before))
    def _():
        halo[:, :edge, :] = jnp.zeros((SIDE, edge, TILE), BF16)

    for j in range(SIDE):
        lanes = slice(j * TILE, (j + 1) * TILE)
        for a in range(atoms):
            first = a * FUNCS * BLOCK
            f = [field[first + i * BLOCK : first + (i + 1) * BLOCK, lanes] for i in range(FUNCS)]
            total = None
            for i in range(FUNCS):
                mixed = ker[i, i, a] * f[i]
                for k in range(i + 1, FUNCS):
                    mixed = mixed + (ker[i, k, a] + ker[k, i, a]) * f[k]
                total = f[i] * mixed if total is None else total + f[i] * mixed
            at = (j * atoms + a) * BLOCK
            dep_rows[at : at + BLOCK, 0:TILE] = total
    dep = dep_rows[...]
    dep_high = dep.astype(BF16)
    dep_low = (dep - dep_high.astype(F32)).astype(BF16)
    loads[2].wait()
    sorted_dep = dot(jnp.concatenate([dep_high, dep_low], axis=1), gather[...]).astype(BF16)

    group = 8 if n % 8 == 0 else n
    span = group * part
    ids = bl[...]
    base = (lax.div(ids, s * blocks) * part + lax.rem(ids, blocks)).astype(F32)
    base = jnp.broadcast_to(base[:, None, :], (atoms, BLOCK, SIDE * SIDE))
    base = base.reshape(atoms * BLOCK, SIDE * SIDE)
    x = lax.broadcasted_iota(jnp.int32, (atoms * BLOCK, 1), 0) % BLOCK
    target = base + ((x % 2) * (n * part) + (x // 2) * blocks).astype(F32)
    index = lax.broadcasted_iota(jnp.int32, (1, 2 * span), 1)
    index = index // span * (n * part) + index % span

    def one_hot(first, zb):
        at = (index + first * part).astype(F32)
        return jnp.concatenate(
            [
                jnp.where(target[:, j * SIDE + zb : j * SIDE + zb + 1] == at, 1.0, 0.0).astype(BF16)
                for j in range(SIDE)
            ],
            axis=0,
        )

    low_half = lax.broadcasted_iota(jnp.int32, (1, 128), 1) < 64

    def deposit_group(g, carry):
        first = g * group
        total = jnp.zeros((2 * span, 128), F32)
        for zb in range(SIDE):
            total = total + dot(
                one_hot(first, zb), sorted_dep[:, zb * 128 : (zb + 1) * 128], ((0,), (0,))
            )
        total = total + pltpu.roll(total, 64, 1)
        dense = jnp.where(low_half, total[:span], total[span:])
        dep_out[pl.ds(first, group)] = dense.reshape(group, part, 128)
        return carry

    if n == group:
        deposit_group(0, 0)
    else:
        lax.fori_loop(0, n // group, deposit_group, 0)

    def send_dep(k, carry):
        peer = lax.rem(me_g + k, n)
        pltpu.make_async_remote_copy(
            src_ref=dep_out.at[peer],
            dst_ref=dep_in.at[k - 1],
            send_sem=dep_send,
            recv_sem=dep_recv,
            device_id=(peer, me_s),
            device_id_type=MESH,
        ).start()
        return carry

    lax.fori_loop(1, n, send_dep, 0)

    loads[4].wait()
    loads[5].wait()
    for j in range(SIDE):
        lanes = slice(j * TILE, (j + 1) * TILE)
        centre = dot(depth[:, 0:rows], fieldb[:, lanes])
        total = centre[:rows] + centre[rows:]
        for which, i in enumerate((j - 1, j, j + 1)):
            if 0 <= i < SIDE:
                f = fieldb[:, i * TILE : (i + 1) * TILE]
                at = which * 2 * TILE
                total = total + dot(f, plane[at : at + TILE, :])
                total = total + dot(f, plane[at + TILE : at + 2 * TILE, :])
        pre[:, lanes] = total

    loads[3].wait()
    pltpu.make_async_copy(
        pot_all.at[pl.ds(0, n - 1)], pot_all.at[pl.ds(0, n - 1)], pot_recv
    ).wait()
    zb_lane = lax.broadcasted_iota(jnp.int32, (1, TILE), 1) // BLOCK % SIDE

    def potential_group(g, total):
        first = g * group
        packed = pot_all[pl.ds(first, group)].reshape(span, 128)
        wide = dot(packed, spread[...]).astype(BF16)
        wide = jnp.concatenate([wide[:, 0:TILE], wide[:, TILE:]], axis=0)
        for zb in range(SIDE):
            found = dot(one_hot(first, zb), wide)
            total = jnp.where(zb_lane == zb, total + found, total)
        return total

    box = jnp.zeros((SIDE * atoms * BLOCK, TILE), F32)
    if n == group:
        box = potential_group(0, box)
    else:
        box = lax.fori_loop(0, n // group, potential_group, box)
    for j in range(SIDE):
        lanes = slice(j * TILE, (j + 1) * TILE)
        here = box[j * atoms * BLOCK : (j + 1) * atoms * BLOCK].reshape(atoms, 1, BLOCK, TILE)
        f = field[:, lanes].reshape(atoms, FUNCS, BLOCK, TILE)
        pre[:, lanes] = pre[:, lanes] + (here * f).reshape(rows, TILE)

    products = jnp.zeros((rows, rows), F32)
    for j in range(SIDE):
        lanes = slice(j * TILE, (j + 1) * TILE)

        @pl.when(has_before)
        def _():
            halo_copy(j, 0).wait_recv()

        @pl.when(has_after)
        def _():
            halo_copy(j, 1).wait_recv()

        outer = dot(depth[:, rows:], halo[j])
        full = pre[:, lanes] + outer[:rows] + outer[rows:]
        full = full.reshape(atoms * FUNCS, BLOCK, TILE)
        full = jnp.where(inside[None, :, lanes], full, 0.0).reshape(rows, TILE)
        high = full.astype(BF16)
        low = (full - high.astype(F32)).astype(BF16)
        applied[:, lanes] = high
        f = fieldb[:, lanes]
        products = products + dot(f, high, ((1,), (1,))) + dot(f, low, ((1,), (1,)))

    group_f = FUNCS * BLOCK
    ri = lax.broadcasted_iota(jnp.int32, (rows, rows), 0)
    ci = lax.broadcasted_iota(jnp.int32, (rows, rows), 1)
    keep = (ri // group_f == ci // group_f) & (ri % BLOCK == ci % BLOCK)
    products = jnp.where(keep, products, 0.0).reshape(atoms, FUNCS, BLOCK, rows)
    by_x = jnp.sum(products, axis=0)
    ham_own[0:FUNCS, :] = jnp.sum(by_x, axis=1)
    ham_own[FUNCS:, :] = jnp.zeros((8 - FUNCS, rows), F32)
    ham_all[pl.ds(me_s, 1)] = ham_own[...][None]
    ham_copies = [
        pltpu.make_async_remote_copy(
            src_ref=ham_own,
            dst_ref=ham_all.at[me_s],
            send_sem=ham_send.at[k],
            recv_sem=ham_recv.at[k],
            device_id=(me_g, lax.rem(me_s + k + 1, s)),
            device_id_type=MESH,
        )
        for k in range(s - 1)
    ]
    for copy in ham_copies:
        copy.start()

    pltpu.make_async_copy(dep_in, dep_in, dep_recv).wait()
    mine = lax.fori_loop(0, n - 1, lambda k, t: t + dep_in[k], dep_out[me_g])
    for c in range(4):
        density[:, c * 128 : (c + 1) * 128] = mine[c * blocks : (c + 1) * blocks]

    for copy in ham_copies:
        copy.wait_recv()
    whole = ham_all[0]
    for k in range(1, s):
        whole = whole + ham_all[k]
    ri = lax.broadcasted_iota(jnp.int32, (rows, FUNCS * 128), 0)
    ci = lax.broadcasted_iota(jnp.int32, (rows, FUNCS * 128), 1)
    fold = (ri // group_f == ci % 128) & (ri // BLOCK % FUNCS == ci // 128)
    whole = dot(whole, jnp.where(fold, CELL_VOLUME, 0.0), precision=lax.Precision.HIGHEST)
    for g in range(FUNCS):
        ham[:, g, :] = whole[0:FUNCS, g * 128 : g * 128 + atoms]

    for copy in ham_copies:
        copy.wait_send()
    pltpu.make_async_copy(
        pot_all.at[pl.ds(0, n - 1)], pot_all.at[pl.ds(0, n - 1)], pot_send
    ).wait()
    pltpu.make_async_copy(dep_in, dep_in, dep_send).wait()

    @pl.when(has_after)
    def _():
        for j in range(SIDE):
            halo_copy(j, 0).wait_send()

    @pl.when(has_before)
    def _():
        for j in range(SIDE):
            halo_copy(j, 1).wait_send()


def per_device(n, s, support, potential, kernel, block_list):
    atoms, _, _, cells = support.shape
    blocks = potential.shape[0]
    rows = atoms * FUNCS * BLOCK
    edge = rows // BLOCK * REACH
    part = blocks * 4
    consts = [jnp.asarray(c) for c in constants(rows)]
    vmem = pl.BlockSpec(memory_space=pltpu.VMEM)
    anywhere = pl.BlockSpec(memory_space=pl.ANY)
    dma = pltpu.SemaphoreType.DMA
    applied, density, ham = pl.pallas_call(
        functools.partial(kernel_body, n, s, atoms, blocks),
        out_shape=(
            jax.ShapeDtypeStruct((rows, cells), BF16),
            jax.ShapeDtypeStruct(potential.shape, F32),
            jax.ShapeDtypeStruct((FUNCS, FUNCS, atoms), F32),
        ),
        in_specs=[
            anywhere, vmem, pl.BlockSpec(memory_space=pltpu.SMEM), vmem,
            *([anywhere] * 5),
        ],
        out_specs=(vmem, vmem, vmem),
        scratch_shapes=[
            pltpu.VMEM((rows, cells), BF16),
            *[pltpu.VMEM(c.shape, BF16) for c in consts],
            pltpu.VMEM((rows, cells), F32),
            pltpu.VMEM((rows, cells), BF16),
            pltpu.VMEM((rows, cells), F32),
            pltpu.VMEM((SIDE, 2 * edge, TILE), BF16),
            pltpu.VMEM((SIDE, 2 * edge, TILE), BF16),
            pltpu.VMEM((part, 128), BF16),
            pltpu.VMEM((n, part, 128), BF16),
            pltpu.VMEM((SIDE * atoms * BLOCK, TILE), F32),
            pltpu.VMEM((n, part, 128), F32),
            pltpu.VMEM((n - 1, part, 128), F32),
            pltpu.VMEM((8, rows), F32),
            pltpu.VMEM((s, 8, rows), F32),
            dma((6,)), dma((2, SIDE)), dma((2, SIDE)), dma, dma, dma, dma,
            dma((s - 1,)), dma((s - 1,)),
        ],
        compiler_params=pltpu.CompilerParams(
            collective_id=0, has_side_effects=True, vmem_limit_bytes=48 * 1024 * 1024
        ),
    )(
        support.reshape(rows, cells),
        potential,
        jnp.transpose(kernel, (1, 2, 0)),
        block_list.reshape(atoms, -1),
        *consts,
    )
    return (
        applied.reshape(support.shape),
        density,
        jnp.transpose(ham, (2, 0, 1)),
    )


def solution(mesh):
    in_specs = (
        P("grid", None, "slab", None),
        P(("grid", "slab"), None),
        P("grid", None, None),
        P("grid", "slab", None),
    )
    out_specs = (P("grid", None, "slab", None), P(("grid", "slab"), None), P("grid", None, None))
    return jax.shard_map(
        functools.partial(per_device, mesh.shape["grid"], mesh.shape["slab"]),
        mesh=mesh, in_specs=in_specs, out_specs=out_specs, check_vma=False,
    )
```

time: 115 us -> 28.4 us (0.25)
  other arithmetic: 32.2 us -> 0 us
  local copies, waits for them, and re-layouts: 40.2 us -> 10.2 us
  starting transfers between devices: 21.9 us -> 0 us
  Pallas kernels: 0 us -> 17.1 us
  blocking collectives: 12.8 us -> 0 us
  matrix products: 6.75 us -> 0 us
    convert_element_type x5 -> x0, other arithmetic: 29 us -> none  [the longest x1 19.6 us: per_device(): applied = applied_full.astype(jnp.bfloat16)]
    all_to_all x3 -> x0, starting transfers between devices: 19.1 us -> none  [the longest x1 7.28 us: per_device(): lax.all_to_all(outgoing_blocks, 'grid', split_axis=0, concat_axis=0, tile...]
    pallas_call x0 -> x1, Pallas kernels: none -> 17.1 us  [per_device(): pl.pallas_call(functools.partial(kernel_body, n, s, atoms, blocks), out_s...]
    reshape x7 -> x0, local copies, waits for them, and re-layouts: 14.9 us -> none  [the longest x1 6.89 us: per_device(): deposit.reshape(atom_count, planes, SIDE_BLOCKS, BLOCK, SIDE_BLOCKS, BLOCK)]
    psum x1 -> x0, blocking collectives: 12.8 us -> none  [per_device(): hamiltonian = lax.psum(local_matrix, 'slab') * CELL_VOLUME]
    unnamed x18 -> x21, local copies, waits for them, and re-layouts: 2.21 us -> 10.2 us
    dot_general x3 -> x0, matrix products: 6.75 us -> none  [the longest x1 3.26 us: per_device(): jnp.einsum('afp,agp->afg', field_flat, applied_full.reshape(atom_count, F...]
    convert_element_type x1 -> x0, local copies, waits for them, and re-layouts: 6.58 us -> none  [per_device(): potential_box.astype(jnp.float32)[:, None] * field_values]
  transfers between devices with their start and end apart: 5 -> 0, of which waited for: 0 -> 0; matrix products, arithmetic and copies ran while one was open for 62% -> 0% of each run, Pallas kernels for 0% -> 0%
where the time goes in v1:
time: 28.4 us; the launch traced here: 28 us
  Pallas kernels  17.1 us (60%)
  local copies, waits for them, and re-layouts  10.2 us (36%)
  between operations  0.66 us (2%)
    pallas_call x1, Pallas kernels, per_device(): pl.pallas_call(functools.partial(kernel_body, n, s, atoms, blocks), out_s...  17.1 us
    unnamed x21, local copies, waits for them, and re-layouts  10.2 us

profile of v1, /device:TPU:0, one launch (start us, length us, event | category | flops | bytes accessed | tf_op | source)
XLA Modules:
  0.0 28.0 jit_solution(6862183792074993077)
XLA Ops:
  0.6 0.0 copy-start.8
  0.6 0.7 %copy-done.8 = s32[8,1,16]{2,1,0:T(1,128)S(1)} copy-done((s32[8,1,16]{2,1,0:T(1,128)S(1)}, s32[8,1,16]{2,1,0:T(1,128)}, u32[]{:S(2)}) %copy-start.8) | copy-done | bytes 536
  1.3 0.0 copy-start
  1.3 1.1 %copy-done = bf16[1536,256]{1,0:T(8,128)(2,1)S(1)} copy-done((bf16[1536,256]{1,0:T(8,128)(2,1)S(1)}, bf16[1536,256]{1,0:T(8,128)(2,1)}, u32[]{:S(2)}) %copy-start) | copy-done | bytes 786456
  2.5 0.0 copy-start.1
  2.5 1.1 %copy-done.1 = bf16[512,640]{1,0:T(8,128)(2,1)S(1)} copy-done((bf16[512,640]{1,0:T(8,128)(2,1)S(1)}, bf16[512,640]{1,0:T(8,128)(2,1)}, u32[]{:S(2)}) %copy-start.1) | copy-done | bytes 655384
  3.5 0.0 copy-start.2
  3.5 1.0 %copy-done.2 = bf16[8,4,8,1024]{3,2,1,0:T(8,128)(2,1)S(1)} copy-done((bf16[8,4,8,1024]{3,2,1,0:T(8,128)(2,1)S(1)}, bf16[8,4,8,1024]{3,2,1,0:T(8,128)(2,1)}, u32[]{:S(2)}) %copy-start.2) | copy-done | bytes 524312
  4.6 0.0 copy-start.3
  4.6 1.0 %copy-done.3 = bf16[512,512]{1,0:T(8,128)(2,1)S(1)} copy-done((bf16[512,512]{1,0:T(8,128)(2,1)S(1)}, bf16[512,512]{1,0:T(8,128)(2,1)}, u32[]{:S(2)}) %copy-start.3) | copy-done | bytes 524312
  5.6 0.0 copy-start.4
  5.6 0.9 %copy-done.4 = bf16[384,256]{1,0:T(8,128)(2,1)S(1)} copy-done((bf16[384,256]{1,0:T(8,128)(2,1)S(1)}, bf16[384,256]{1,0:T(8,128)(2,1)}, u32[]{:S(2)}) %copy-start.4) | copy-done | bytes 196632
  6.6 0.0 copy-start.5
  6.6 0.9 %copy-done.5 = bf16[128,512]{1,0:T(8,128)(2,1)S(1)} copy-done((bf16[128,512]{1,0:T(8,128)(2,1)S(1)}, bf16[128,512]{1,0:T(8,128)(2,1)}, u32[]{:S(2)}) %copy-start.5) | copy-done | bytes 131096
  7.5 0.0 copy-start.6
  7.5 0.7 %copy-done.6 = bf16[8,512]{1,0:T(8,128)(2,1)S(1)} copy-done((bf16[8,512]{1,0:T(8,128)(2,1)S(1)}, bf16[8,512]{1,0:T(8,128)(2,1)}, u32[]{:S(2)}) %copy-start.6) | copy-done | bytes 8216
  8.2 0.0 copy-start.7
  8.2 0.7 %copy-done.7 = f32[8,4,4]{0,2,1:T(4,128)S(1)} copy-done((f32[8,4,4]{0,2,1:T(4,128)S(1)}, f32[8,4,4]{0,2,1:T(4,128)}, u32[]{:S(2)}) %copy-start.7) | copy-done | bytes 536
  8.9 17.1 %shard_map.112 = (bf16[256,1024]{1,0:T(8,128)(2,1)S(1)}, f32[8,512]{1,0:T(8,128)S(1)}, f32[4,4,8]{2,1,0:T(4,128)S(1)}) custom-call(bf16[256,1024]{1,0:T(8,128)(2,1)S(1)} %bitcast.6, bf16[8,512]{1,0:T(8,128)(2,1)S(1)} %copy-done.6, f32[4,4,8]{2,1,0:T(4,128)S(1)} %bitcast.7, s32[8,16]{1,0:T(8,128)S(1)} %bitcast.9, bf16[1536,256]{1,0:T(8,128)(2,1)S(1)} %copy-done, ...), custom_call_target="tpu_custom_call" | custom-call | tf_op jit(solution)/shard_map/pallas_call | solution.py:413
  26.0 0.8 %copy.15 = bf16[8,4,8,1024]{3,2,1,0:T(8,128)(2,1)} copy(bf16[8,4,8,1024]{3,2,1,0:T(8,128)(2,1)S(1)} %bitcast.5) | data formatting | bytes 1048576
  26.8 0.6 %copy.16 = f32[8,512]{1,0:T(8,128)} copy(f32[8,512]{1,0:T(8,128)S(1)} %get-tuple-element.13) | data formatting | bytes 32768
  27.4 0.6 %copy.17 = f32[8,4,4]{0,2,1:T(4,128)} copy(f32[8,4,4]{0,2,1:T(4,128)S(1)} %bitcast.8) | data formatting | bytes 1024
Async XLA Ops:
  0.6 0.7 %copy-start.8 = (s32[8,1,16]{2,1,0:T(1,128)S(1)}, s32[8,1,16]{2,1,0:T(1,128)}, u32[]{:S(2)}) copy-start(s32[8,1,16]{2,1,0:T(1,128)} %param.12) | copy-start | bytes 1540
  1.3 1.1 %copy-start = (bf16[1536,256]{1,0:T(8,128)(2,1)S(1)}, bf16[1536,256]{1,0:T(8,128)(2,1)}, u32[]{:S(2)}) copy-start(bf16[1536,256]{1,0:T(8,128)(2,1)} %constant.10.clone.plane_hbm) | copy-start | bytes 2359300
  2.5 1.1 %copy-start.1 = (bf16[512,640]{1,0:T(8,128)(2,1)S(1)}, bf16[512,640]{1,0:T(8,128)(2,1)}, u32[]{:S(2)}) copy-start(bf16[512,640]{1,0:T(8,128)(2,1)} %constant.11.clone.depth_hbm) | copy-start | bytes 1966084
  3.5 1.0 %copy-start.2 = (bf16[8,4,8,1024]{3,2,1,0:T(8,128)(2,1)S(1)}, bf16[8,4,8,1024]{3,2,1,0:T(8,128)(2,1)}, u32[]{:S(2)}) copy-start(bf16[8,4,8,1024]{3,2,1,0:T(8,128)(2,1)} %param.9) | copy-start | bytes 1572868
  4.6 1.0 %copy-start.3 = (bf16[512,512]{1,0:T(8,128)(2,1)S(1)}, bf16[512,512]{1,0:T(8,128)(2,1)}, u32[]{:S(2)}) copy-start(bf16[512,512]{1,0:T(8,128)(2,1)} %constant.14.clone.gather_hbm) | copy-start | bytes 1572868
  5.6 0.9 %copy-start.4 = (bf16[384,256]{1,0:T(8,128)(2,1)S(1)}, bf16[384,256]{1,0:T(8,128)(2,1)}, u32[]{:S(2)}) copy-start(bf16[384,256]{1,0:T(8,128)(2,1)} %constant.12.clone.select_hbm) | copy-start | bytes 589828
  6.6 0.9 %copy-start.5 = (bf16[128,512]{1,0:T(8,128)(2,1)S(1)}, bf16[128,512]{1,0:T(8,128)(2,1)}, u32[]{:S(2)}) copy-start(bf16[128,512]{1,0:T(8,128)(2,1)} %constant.13.clone.spread_hbm) | copy-start | bytes 393220
  7.5 0.7 %copy-start.6 = (bf16[8,512]{1,0:T(8,128)(2,1)S(1)}, bf16[8,512]{1,0:T(8,128)(2,1)}, u32[]{:S(2)}) copy-start(bf16[8,512]{1,0:T(8,128)(2,1)} %pot.1) | copy-start | bytes 24580
  8.2 0.7 %copy-start.7 = (f32[8,4,4]{0,2,1:T(4,128)S(1)}, f32[8,4,4]{0,2,1:T(4,128)}, u32[]{:S(2)}) copy-start(f32[8,4,4]{0,2,1:T(4,128)} %param.11) | copy-start | bytes 1540

commit v2 on v1

--- a/solution.py
+++ b/solution.py
@@ -83,8 +83,16 @@
     here = (y[:, None] == (goal // 8)[None]) & (z[:, None] == (slot * 8 + goal % 8)[None])
     gather = np.concatenate([here & (side == h)[None] for h in (0, 1)], axis=0)
 
+    group = FUNCS * BLOCK
+    keep = (row // group)[:, None] == (row // group)[None]
+    keep = keep & (x[:, None] == x[None])
+    lane = np.arange(128)
+    fold = (row // group)[:, None] == (lane % 32)[None]
+    fold = fold & ((pair % FUNCS)[:, None] == (lane // 32)[None])
+    pick = np.concatenate([keep, CELL_VOLUME * fold], axis=1)
+
     to = ml_dtypes.bfloat16
-    return plane, depth, select.astype(to), spread.astype(to), gather.astype(to)
+    return plane, depth, *[c.astype(to) for c in (select, spread, gather, pick)]
 
 
 def dot(a, b, dims=((1,), (0,)), precision=None):
@@ -95,12 +103,12 @@
 
 def kernel_body(
     n, s, atoms, blocks,
-    sup_hbm, pot, ker, bl, plane_hbm, depth_hbm, select_hbm, spread_hbm, gather_hbm,
-    applied, density, ham,
-    sup, plane, depth, select, spread, gather,
+    sup_hbm, pot_hbm, ker_hbm, bl_hbm, plane_hbm, depth_hbm, select_hbm, spread_hbm, gather_hbm, pick_hbm,
+    applied_hbm, density_hbm, ham_all,
+    sup, pot, ker, bl, plane, depth, select, spread, gather, pick,
     field, fieldb, pre, halo_out, halo, pot_own, pot_all, dep_rows, dep_out, dep_in,
-    ham_own, ham_all,
-    load_sem, halo_send, halo_recv, pot_send, pot_recv, dep_send, dep_recv,
+    ham_own, chosen, applied, density,
+    load_sem, store_sem, halo_send, halo_recv, pot_send, pot_recv, dep_send, dep_recv,
     ham_send, ham_recv,
 ):
     rows = atoms * FUNCS * BLOCK
@@ -114,12 +122,14 @@
             (
                 (sup_hbm, sup), (select_hbm, select), (gather_hbm, gather),
                 (spread_hbm, spread), (plane_hbm, plane), (depth_hbm, depth),
+                (pot_hbm, pot), (ker_hbm, ker), (bl_hbm, bl), (pick_hbm, pick),
             )
         )
     ]
-    for load in loads:
-        load.start()
-
+    for i in (0, 6, 1, 7, 8, 2, 5, 4, 3, 9):
+        loads[i].start()
+
+    ham_own[...] = jnp.zeros(ham_own.shape, F32)
     barrier = pltpu.get_barrier_semaphore()
 
     def greet(k, carry):
@@ -134,6 +144,7 @@
             barrier, inc=1, device_id=(me_g, lax.rem(me_s + k, s)), device_id_type=MESH
         )
 
+    loads[6].wait()
     own = pot[...].astype(F32)
     for c in range(4):
         dep_rows[c * blocks : (c + 1) * blocks, 0:128] = own[:, c * 128 : (c + 1) * 128]
@@ -173,7 +184,6 @@
         pot_copy(k).start()
         return carry
 
-    lax.fori_loop(1, n, send_pot, 0)
 
     def halo_copy(j, direction):
         first = direction * edge
@@ -198,6 +208,8 @@
         for j in range(SIDE):
             halo_copy(j, 1).start()
 
+    lax.fori_loop(1, n, send_pot, 0)
+
     @pl.when(jnp.logical_not(has_after))
     def _():
         halo[:, edge:, :] = jnp.zeros((SIDE, edge, TILE), BF16)
@@ -206,6 +218,7 @@
     def _():
         halo[:, :edge, :] = jnp.zeros((SIDE, edge, TILE), BF16)
 
+    loads[7].wait()
     for j in range(SIDE):
         lanes = slice(j * TILE, (j + 1) * TILE)
         for a in range(atoms):
@@ -227,6 +240,7 @@
 
     group = 8 if n % 8 == 0 else n
     span = group * part
+    loads[8].wait()
     ids = bl[...]
     base = (lax.div(ids, s * blocks) * part + lax.rem(ids, blocks)).astype(F32)
     base = jnp.broadcast_to(base[:, None, :], (atoms, BLOCK, SIDE * SIDE))
@@ -248,12 +262,19 @@
 
     low_half = lax.broadcasted_iota(jnp.int32, (1, 128), 1) < 64
 
+    if n == group:
+        for zb in range(SIDE):
+            chosen[zb] = one_hot(0, zb)
+
+    def choice(first, zb):
+        return chosen[zb] if n == group else one_hot(first, zb)
+
     def deposit_group(g, carry):
         first = g * group
         total = jnp.zeros((2 * span, 128), F32)
         for zb in range(SIDE):
             total = total + dot(
-                one_hot(first, zb), sorted_dep[:, zb * 128 : (zb + 1) * 128], ((0,), (0,))
+                choice(first, zb), sorted_dep[:, zb * 128 : (zb + 1) * 128], ((0,), (0,))
             )
         total = total + pltpu.roll(total, 64, 1)
         dense = jnp.where(low_half, total[:span], total[span:])
@@ -305,7 +326,7 @@
         wide = dot(packed, spread[...]).astype(BF16)
         wide = jnp.concatenate([wide[:, 0:TILE], wide[:, TILE:]], axis=0)
         for zb in range(SIDE):
-            found = dot(one_hot(first, zb), wide)
+            found = dot(choice(first, zb), wide)
             total = jnp.where(zb_lane == zb, total + found, total)
         return total
 
@@ -321,6 +342,7 @@
         pre[:, lanes] = pre[:, lanes] + (here * f).reshape(rows, TILE)
 
     products = jnp.zeros((rows, rows), F32)
+    stores = []
     for j in range(SIDE):
         lanes = slice(j * TILE, (j + 1) * TILE)
 
@@ -339,18 +361,30 @@
         high = full.astype(BF16)
         low = (full - high.astype(F32)).astype(BF16)
         applied[:, lanes] = high
+        stores.append(
+            pltpu.make_async_copy(
+                applied.at[:, pl.ds(j * TILE, TILE)],
+                applied_hbm.at[:, pl.ds(j * TILE, TILE)],
+                store_sem.at[j],
+            )
+        )
+        stores[j].start()
         f = fieldb[:, lanes]
         products = products + dot(f, high, ((1,), (1,))) + dot(f, low, ((1,), (1,)))
 
-    group_f = FUNCS * BLOCK
-    ri = lax.broadcasted_iota(jnp.int32, (rows, rows), 0)
-    ci = lax.broadcasted_iota(jnp.int32, (rows, rows), 1)
-    keep = (ri // group_f == ci // group_f) & (ri % BLOCK == ci % BLOCK)
-    products = jnp.where(keep, products, 0.0).reshape(atoms, FUNCS, BLOCK, rows)
-    by_x = jnp.sum(products, axis=0)
-    ham_own[0:FUNCS, :] = jnp.sum(by_x, axis=1)
-    ham_own[FUNCS:, :] = jnp.zeros((8 - FUNCS, rows), F32)
-    ham_all[pl.ds(me_s, 1)] = ham_own[...][None]
+    loads[9].wait()
+    products = products * pick[:, 0:rows].astype(F32)
+    products = jnp.sum(products.reshape(atoms, FUNCS, BLOCK, rows), axis=0)
+    rest = jnp.sum(products, axis=1)
+    terms = []
+    for _ in range(3):
+        terms.append(rest.astype(BF16).astype(F32))
+        rest = rest - terms[-1]
+    terms = jnp.concatenate(terms + [rest], axis=0).astype(BF16)
+    folded = dot(terms, pick[:, rows:])
+    ham_own[0:FUNCS, :] = (folded[8:12] + folded[4:8]) + folded[0:4]
+    stores.append(pltpu.make_async_copy(ham_own, ham_all.at[me_s], store_sem.at[SIDE]))
+    stores[SIDE].start()
     ham_copies = [
         pltpu.make_async_remote_copy(
             src_ref=ham_own,
@@ -369,18 +403,11 @@
     mine = lax.fori_loop(0, n - 1, lambda k, t: t + dep_in[k], dep_out[me_g])
     for c in range(4):
         density[:, c * 128 : (c + 1) * 128] = mine[c * blocks : (c + 1) * blocks]
+    stores.append(pltpu.make_async_copy(density, density_hbm, store_sem.at[SIDE + 1]))
+    stores[SIDE + 1].start()
 
     for copy in ham_copies:
         copy.wait_recv()
-    whole = ham_all[0]
-    for k in range(1, s):
-        whole = whole + ham_all[k]
-    ri = lax.broadcasted_iota(jnp.int32, (rows, FUNCS * 128), 0)
-    ci = lax.broadcasted_iota(jnp.int32, (rows, FUNCS * 128), 1)
-    fold = (ri // group_f == ci % 128) & (ri // BLOCK % FUNCS == ci // 128)
-    whole = dot(whole, jnp.where(fold, CELL_VOLUME, 0.0), precision=lax.Precision.HIGHEST)
-    for g in range(FUNCS):
-        ham[:, g, :] = whole[0:FUNCS, g * 128 : g * 128 + atoms]
 
     for copy in ham_copies:
         copy.wait_send()
@@ -398,6 +425,34 @@
     def _():
         for j in range(SIDE):
             halo_copy(j, 1).wait_send()
+
+    for store in stores:
+        store.wait()
+
+
+def store_body(a, b, c, a_out, b_out, c_out, a_mid, b_mid, c_mid, ham, load_sem, store_sem):
+    step = a.shape[0] // SIDE
+    moves = [(c, c_mid, None), (b, b_mid, b_out)]
+    for i in range(SIDE):
+        at = pl.ds(i * step, step)
+        moves.append((a.at[at], a_mid.at[at], a_out.at[at]))
+    loads = [pltpu.make_async_copy(m[0], m[1], load_sem.at[i]) for i, m in enumerate(moves)]
+    for load in loads:
+        load.start()
+    loads[0].wait()
+    whole = c_mid[0]
+    for k in range(1, c_mid.shape[0]):
+        whole = whole + c_mid[k]
+    for g in range(FUNCS):
+        ham[:, g, :] = whole[0:FUNCS, g * 32 : g * 32 + ham.shape[2]]
+    stores = [pltpu.make_async_copy(ham, c_out, store_sem.at[0])]
+    stores[0].start()
+    for i in range(1, SIDE + 2):
+        loads[i].wait()
+        stores.append(pltpu.make_async_copy(moves[i][1], moves[i][2], store_sem.at[i]))
+        stores[i].start()
+    for store in stores:
+        store.wait()
 
 
 def per_device(n, s, support, potential, kernel, block_list):
@@ -407,23 +462,22 @@
     edge = rows // BLOCK * REACH
     part = blocks * 4
     consts = [jnp.asarray(c) for c in constants(rows)]
-    vmem = pl.BlockSpec(memory_space=pltpu.VMEM)
-    anywhere = pl.BlockSpec(memory_space=pl.ANY)
+    hbm = pl.BlockSpec(memory_space=pltpu.HBM)
     dma = pltpu.SemaphoreType.DMA
     applied, density, ham = pl.pallas_call(
         functools.partial(kernel_body, n, s, atoms, blocks),
         out_shape=(
             jax.ShapeDtypeStruct((rows, cells), BF16),
             jax.ShapeDtypeStruct(potential.shape, F32),
-            jax.ShapeDtypeStruct((FUNCS, FUNCS, atoms), F32),
+            jax.ShapeDtypeStruct((s, 8, 128), F32),
         ),
-        in_specs=[
-            anywhere, vmem, pl.BlockSpec(memory_space=pltpu.SMEM), vmem,
-            *([anywhere] * 5),
-        ],
-        out_specs=(vmem, vmem, vmem),
+        in_specs=[hbm] * 10,
+        out_specs=(hbm, hbm, hbm),
         scratch_shapes=[
             pltpu.VMEM((rows, cells), BF16),
+            pltpu.VMEM(potential.shape, BF16),
+            pltpu.SMEM((FUNCS, FUNCS, atoms), F32),
+            pltpu.VMEM((atoms, SIDE * SIDE), jnp.int32),
             *[pltpu.VMEM(c.shape, BF16) for c in consts],
             pltpu.VMEM((rows, cells), F32),
             pltpu.VMEM((rows, cells), BF16),
@@ -435,13 +489,15 @@
             pltpu.VMEM((SIDE * atoms * BLOCK, TILE), F32),
             pltpu.VMEM((n, part, 128), F32),
             pltpu.VMEM((n - 1, part, 128), F32),
-            pltpu.VMEM((8, rows), F32),
-            pltpu.VMEM((s, 8, rows), F32),
-            dma((6,)), dma((2, SIDE)), dma((2, SIDE)), dma, dma, dma, dma,
+            pltpu.VMEM((8, 128), F32),
+            pltpu.VMEM((SIDE, SIDE * atoms * BLOCK, 2 * min(n, 8) * part), BF16),
+            pltpu.VMEM((rows, cells), BF16),
+            pltpu.VMEM(potential.shape, F32),
+            dma((10,)), dma((SIDE + 2,)), dma((2, SIDE)), dma((2, SIDE)), dma, dma, dma, dma,
             dma((s - 1,)), dma((s - 1,)),
         ],
         compiler_params=pltpu.CompilerParams(
-            collective_id=0, has_side_effects=True, vmem_limit_bytes=48 * 1024 * 1024
+            collective_id=0, has_side_effects=True, vmem_limit_bytes=64 * 1024 * 1024
         ),
     )(
         support.reshape(rows, cells),
@@ -450,6 +506,24 @@
         block_list.reshape(atoms, -1),
         *consts,
     )
+    results = (applied, density, ham)
+    matrix = jax.ShapeDtypeStruct((FUNCS, FUNCS, atoms), F32)
+    applied, density, ham = pl.pallas_call(
+        store_body,
+        out_shape=(
+            jax.ShapeDtypeStruct((rows, cells), BF16),
+            jax.ShapeDtypeStruct(potential.shape, F32),
+            matrix,
+        ),
+        in_specs=[hbm] * 3,
+        out_specs=(hbm,) * 3,
+        scratch_shapes=[
+            *[pltpu.VMEM(r.shape, r.dtype) for r in results],
+            pltpu.VMEM(matrix.shape, F32),
+            dma((SIDE + 2,)), dma((SIDE + 2,)),
+        ],
+        compiler_params=pltpu.CompilerParams(vmem_limit_bytes=64 * 1024 * 1024),
+    )(*results)
     return (
         applied.reshape(support.shape),
         density,

time: 28.4 us -> 18.9 us (0.67)
  local copies, waits for them, and re-layouts: 10.2 us -> 0 us
  Pallas kernels: 17.1 us -> 18.1 us
    unnamed x21 -> x0, local copies, waits for them, and re-layouts: 10.2 us -> none
    pallas_call x0 -> x1, Pallas kernels: none -> 1.89 us  [per_device(): pl.pallas_call(store_body, out_shape=(jax.ShapeDtypeStruct((rows, cells),...]
    pallas_call x1, Pallas kernels: 17.1 us -> 16.2 us  [per_device(): pl.pallas_call(functools.partial(kernel_body, n, s, atoms, blocks), out_s...]
where the time goes in v2:
time: 18.9 us; the launch traced here: 18.7 us
  Pallas kernels  18.1 us (96%)
  between operations  0.64 us (3%)
    pallas_call x1, Pallas kernels, per_device(): pl.pallas_call(functools.partial(kernel_body, n, s, atoms, blocks), out_s...  16.2 us
    pallas_call x1, Pallas kernels, per_device(): pl.pallas_call(store_body, out_shape=(jax.ShapeDtypeStruct((rows, cells),...  1.89 us

profile of v2, /device:TPU:0, one launch (start us, length us, event | category | flops | bytes accessed | tf_op | source)
XLA Modules:
  0.0 18.7 jit_solution(16001216856467273418)
XLA Ops:
  0.6 16.2 %shard_map.121 = (bf16[256,1024]{1,0:T(8,128)(2,1)}, f32[8,512]{1,0:T(8,128)}, f32[4,8,128]{2,1,0:T(8,128)}) custom-call(bf16[256,1024]{1,0:T(8,128)(2,1)} %bitcast.5, bf16[8,512]{1,0:T(8,128)(2,1)} %pot_hbm.1, f32[4,4,8]{2,1,0:T(4,128)} %bitcast.6, s32[8,16]{1,0:T(8,128)} %bitcast.7, bf16[1536,256]{1,0:T(8,128)(2,1)} %constant.12.clone.plane_hbm, ...), custom_call_target="tpu_custom_call" | custom-call | tf_op jit(solution)/shard_map/pallas_call | solution.py:467
  16.8 1.9 %shard_map.122 = (bf16[256,1024]{1,0:T(8,128)(2,1)}, f32[8,512]{1,0:T(8,128)}, f32[4,4,8]{2,1,0:T(4,128)}) custom-call(bf16[256,1024]{1,0:T(8,128)(2,1)} %get-tuple-element.9.a, f32[8,512]{1,0:T(8,128)} %get-tuple-element.10.b, f32[4,8,128]{2,1,0:T(8,128)} %get-tuple-element.11.c), custom_call_target="tpu_custom_call" | custom-call | tf_op jit(solution)/shard_map/pallas_call | solution.py:511

commit v3 on v2

--- a/solution.py
+++ b/solution.py
@@ -15,6 +15,7 @@
 RADIUS = 13
 SIDE = 4
 REACH = 6
+WIDE = 2
 TILE = 256
 WEIGHTS = (
     -5369.0 / 1800.0,
@@ -126,7 +127,7 @@
             )
         )
     ]
-    for i in (0, 6, 1, 7, 8, 2, 5, 4, 3, 9):
+    for i in (0, 6, 1, 7, 8):
         loads[i].start()
 
     ham_own[...] = jnp.zeros(ham_own.shape, F32)
@@ -163,6 +164,8 @@
         values = jnp.where(inside[None, :, lanes], values, 0.0).reshape(rows, TILE)
         field[:, lanes] = values
         fieldb[:, lanes] = values.astype(BF16)
+    for i in (2, 5, 4, 3, 9):
+        loads[i].start()
     loads[1].wait()
     for j in range(SIDE):
         lanes = slice(j * TILE, (j + 1) * TILE)
@@ -185,11 +188,13 @@
         return carry
 
 
+    lax.fori_loop(1, n, send_pot, 0)
+
     def halo_copy(j, direction):
         first = direction * edge
         return pltpu.make_async_remote_copy(
-            src_ref=halo_out.at[j, pl.ds(first, edge)],
-            dst_ref=halo.at[j, pl.ds(first, edge)],
+            src_ref=halo_out.at[pl.ds(j * WIDE, WIDE), pl.ds(first, edge)],
+            dst_ref=halo.at[pl.ds(j * WIDE, WIDE), pl.ds(first, edge)],
             send_sem=halo_send.at[direction, j],
             recv_sem=halo_recv.at[direction, j],
             device_id=(me_g, me_s + 1 - 2 * direction),
@@ -200,15 +205,13 @@
 
     @pl.when(has_after)
     def _():
-        for j in range(SIDE):
+        for j in range(SIDE // WIDE):
             halo_copy(j, 0).start()
 
     @pl.when(has_before)
     def _():
-        for j in range(SIDE):
+        for j in range(SIDE // WIDE):
             halo_copy(j, 1).start()
-
-    lax.fori_loop(1, n, send_pot, 0)
 
     @pl.when(jnp.logical_not(has_after))
     def _():
@@ -346,13 +349,15 @@
     for j in range(SIDE):
         lanes = slice(j * TILE, (j + 1) * TILE)
 
-        @pl.when(has_before)
-        def _():
-            halo_copy(j, 0).wait_recv()
-
-        @pl.when(has_after)
-        def _():
-            halo_copy(j, 1).wait_recv()
+        if j % WIDE == 0:
+
+            @pl.when(has_before)
+            def _():
+                halo_copy(j // WIDE, 0).wait_recv()
+
+            @pl.when(has_after)
+            def _():
+                halo_copy(j // WIDE, 1).wait_recv()
 
         outer = dot(depth[:, rows:], halo[j])
         full = pre[:, lanes] + outer[:rows] + outer[rows:]
@@ -418,12 +423,12 @@
 
     @pl.when(has_after)
     def _():
-        for j in range(SIDE):
+        for j in range(SIDE // WIDE):
             halo_copy(j, 0).wait_send()
 
     @pl.when(has_before)
     def _():
-        for j in range(SIDE):
+        for j in range(SIDE // WIDE):
             halo_copy(j, 1).wait_send()
 
     for store in stores:

time: 18.9 us -> 18.6 us (0.984)
  Pallas kernels: 18.1 us -> 17.7 us
    pallas_call x1, Pallas kernels: 16.2 us -> 15.8 us  [per_device(): pl.pallas_call(functools.partial(kernel_body, n, s, atoms, blocks), out_s...]
where the time goes in v3:
time: 18.6 us; the launch traced here: 18.3 us
  Pallas kernels  17.7 us (95%)
  between operations  0.64 us (3%)
    pallas_call x1, Pallas kernels, per_device(): pl.pallas_call(functools.partial(kernel_body, n, s, atoms, blocks), out_s...  15.8 us
    pallas_call x1, Pallas kernels, per_device(): pl.pallas_call(store_body, out_shape=(jax.ShapeDtypeStruct((rows, cells),...  1.89 us

profile of v3, /device:TPU:0, one launch (start us, length us, event | category | flops | bytes accessed | tf_op | source)
XLA Modules:
  0.0 18.3 jit_solution(14533825438370241900)
XLA Ops:
  0.6 15.8 %shard_map.121 = (bf16[256,1024]{1,0:T(8,128)(2,1)}, f32[8,512]{1,0:T(8,128)}, f32[4,8,128]{2,1,0:T(8,128)}) custom-call(bf16[256,1024]{1,0:T(8,128)(2,1)} %bitcast.5, bf16[8,512]{1,0:T(8,128)(2,1)} %pot_hbm.1, f32[4,4,8]{2,1,0:T(4,128)} %bitcast.6, s32[8,16]{1,0:T(8,128)} %bitcast.7, bf16[1536,256]{1,0:T(8,128)(2,1)} %constant.12.clone.plane_hbm, ...), custom_call_target="tpu_custom_call" | custom-call | tf_op jit(solution)/shard_map/pallas_call | solution.py:472
  16.4 1.9 %shard_map.122 = (bf16[256,1024]{1,0:T(8,128)(2,1)}, f32[8,512]{1,0:T(8,128)}, f32[4,4,8]{2,1,0:T(4,128)}) custom-call(bf16[256,1024]{1,0:T(8,128)(2,1)} %get-tuple-element.9.a, f32[8,512]{1,0:T(8,128)} %get-tuple-element.10.b, f32[4,8,128]{2,1,0:T(8,128)} %get-tuple-element.11.c), custom_call_target="tpu_custom_call" | custom-call | tf_op jit(solution)/shard_map/pallas_call | solution.py:516

commit v4 on v3

--- a/solution.py
+++ b/solution.py
@@ -197,7 +197,7 @@
             dst_ref=halo.at[pl.ds(j * WIDE, WIDE), pl.ds(first, edge)],
             send_sem=halo_send.at[direction, j],
             recv_sem=halo_recv.at[direction, j],
-            device_id=(me_g, me_s + 1 - 2 * direction),
+            device_id=(me_g, lax.rem(me_s + s + 1 - 2 * direction, s)),
             device_id_type=MESH,
         )
 

time: 18.6 us -> 18.6 us (level)
  no operation moved by 1% of the time
where the time goes in v4:
time: 18.6 us; the launch traced here: 18.3 us
  Pallas kernels  17.7 us (95%)
  between operations  0.64 us (3%)
    pallas_call x1, Pallas kernels, per_device(): pl.pallas_call(functools.partial(kernel_body, n, s, atoms, blocks), out_s...  15.8 us
    pallas_call x1, Pallas kernels, per_device(): pl.pallas_call(store_body, out_shape=(jax.ShapeDtypeStruct((rows, cells),...  1.89 us

profile of v4, /device:TPU:0, one launch (start us, length us, event | category | flops | bytes accessed | tf_op | source)
XLA Modules:
  0.0 18.3 jit_solution(6672309002469502579)
XLA Ops:
  0.6 15.8 %shard_map.121 = (bf16[256,1024]{1,0:T(8,128)(2,1)}, f32[8,512]{1,0:T(8,128)}, f32[4,8,128]{2,1,0:T(8,128)}) custom-call(bf16[256,1024]{1,0:T(8,128)(2,1)} %bitcast.5, bf16[8,512]{1,0:T(8,128)(2,1)} %pot_hbm.1, f32[4,4,8]{2,1,0:T(4,128)} %bitcast.6, s32[8,16]{1,0:T(8,128)} %bitcast.7, bf16[1536,256]{1,0:T(8,128)(2,1)} %constant.12.clone.plane_hbm, ...), custom_call_target="tpu_custom_call" | custom-call | tf_op jit(solution)/shard_map/pallas_call | solution.py:472
  16.4 1.9 %shard_map.122 = (bf16[256,1024]{1,0:T(8,128)(2,1)}, f32[8,512]{1,0:T(8,128)}, f32[4,4,8]{2,1,0:T(4,128)}) custom-call(bf16[256,1024]{1,0:T(8,128)(2,1)} %get-tuple-element.9.a, f32[8,512]{1,0:T(8,128)} %get-tuple-element.10.b, f32[4,8,128]{2,1,0:T(8,128)} %get-tuple-element.11.c), custom_call_target="tpu_custom_call" | custom-call | tf_op jit(solution)/shard_map/pallas_call | solution.py:516
